TPU v7x, 32 devices: a whole 2x2x4 slice. The times are simulated.
32 devices in a mesh: layer: 4 (over z), row: 2 (over x), col: 4 (over y, core).
Axes of the slice: x: 2, y: 2, z: 4, core: 2. Of those that a mesh axis runs over, the one named last changes fastest.
Arguments:
- density: float32 [1024, 1024], P(('row', 'col'), 'layer'), as said below
- pattern: int32 [8, 8], replicated, may hold values from 0 to 1, as said below
Outputs:
- purified: float32 [1024, 1024], P(('row', 'col'), 'layer')
Inputs may be any that keep to these rules, and one draw needn't show every extreme that they name: pattern is symmetric, its diagonal is all ones. density is symmetric.
All inputs are finite; a program needn't handle non-finite values.
Results may differ from a plain program's by a relative error of at most 0.00013.
Values sent between devices are 32-bit elements; how exact they have to be, the bound alone decides.
A program may use at most 64 MiB of HBM per device.

v0:
```python
import jax
import jax.numpy as jnp
from jax import lax
from jax.sharding import PartitionSpec as P

TILE = 128


def times_panel(left, panel):
    return lax.dot_general(
        left,
        panel,
        (((1,), (1,)), ((), ())),
        precision=lax.Precision.HIGHEST,
        preferred_element_type=jnp.float32,
    )


def times_rows(left, panel):
    return jnp.dot(left, panel, precision=lax.Precision.HIGHEST, preferred_element_type=jnp.float32)


def on_device(density, pattern):
    row_count, col_count = density.shape
    tile_rows = row_count // TILE
    tile_cols = col_count // TILE
    row_start = lax.axis_index(("row", "col")) * tile_rows
    col_start = lax.axis_index("layer") * tile_cols
    local_keep = lax.dynamic_slice(pattern, (row_start, col_start), (tile_rows, tile_cols)).astype(
        jnp.float32
    )
    expanded = jnp.broadcast_to(
        local_keep[:, None, :, None], (tile_rows, TILE, tile_cols, TILE)
    ).reshape(row_count, col_count)
    masked = density * expanded
    gathered = lax.all_gather(masked, ("row", "col"), axis=0, tiled=True)
    partial_value = times_panel(masked, gathered)
    whole_rows = lax.psum(partial_value, "layer")
    square = lax.dynamic_slice_in_dim(whole_rows, lax.axis_index("layer") * col_count, col_count, 1)
    cube = times_rows(whole_rows, gathered)
    return 3.0 * square - 2.0 * cube


def solution(mesh):
    return jax.shard_map(
        on_device,
        mesh=mesh,
        in_specs=(P(("row", "col"), "layer"), P()),
        out_specs=P(("row", "col"), "layer"),
        check_vma=False,
    )
```

profile of v0, /device:TPU:0, one launch (start us, length us, event | category | flops | bytes accessed | tf_op | source)
XLA Modules:
  0.0 86.4 jit_solution(6384011395737866362)
XLA Ops:
  6.5 0.0 all-gather.2.cloned.1.call-start
  6.5 0.8 convert_bitcast_fusion
  7.3 0.1 broadcast_bitcast_fusion
  7.4 1.6 %broadcast_multiply_fusion = f32[128,256]{1,0:T(8,128)} fusion(f32[128,256]{1,0:T(8,128)} %param.2, f32[256]{0:T(256)S(1)} %broadcast_bitcast_fusion), kind=kLoop, calls=%fused_computation.2 | loop fusion | flops 32768 | bytes 263168 | tf_op jit(solution)/shard_map/mul | solution.py:35
  8.9 0.0 copy-start.1
  8.9 0.0 all-gather.2.cloned.1.call-update
  9.0 0.0 all-reduce.2.cloned.1.call-start
  9.0 26.5 %all-gather.2.cloned.1.call-done = f32[1024,256]{1,0:T(8,128)} async-done(((f32[128,256]{1,0:T(8,128)}), f32[1024,256]{1,0:T(8,128)}) %all-gather.2.cloned.1.call-update) | async-done | bytes 1048592 | tf_op jit(solution)/shard_map/all_gather | solution.py:36
  35.5 0.0 copy-done.1
  35.5 0.0 copy-start
  35.5 3.3 %fusion.1 = f32[128,1024]{1,0:T(8,128)} fusion(f32[128,256]{1,0:T(8,128)S(1)} %copy-done.1, f32[1024,256]{1,0:T(8,128)} %all-gather.2.cloned.1.call-done), kind=kOutput, calls=%fused_computation.5 | convolution fusion | flops 402653184 | bytes 1703936 | tf_op jit(solution)/shard_map/dot_general | solution.py:10
  38.8 0.0 all-reduce.2.cloned.1.call-update
  38.8 38.4 %all-reduce.2.cloned.1.call-done = f32[128,1024]{1,0:T(8,128)} async-done(((f32[128,1024]{1,0:T(8,128)}), f32[128,1024]{1,0:T(8,128)}) %all-reduce.2.cloned.1.call-update) | async-done | bytes 524304 | tf_op jit(solution)/shard_map/psum | solution.py:38
  77.2 0.0 copy-done
  77.2 2.4 %fusion = f32[128,256]{1,0:T(8,128)} fusion(f32[128,1024]{1,0:T(8,128)} %all-reduce.2.cloned.1.call-done, f32[1024,256]{1,0:T(8,128)S(1)} %copy-done, s32[]{:T(128)S(6)} %select_n.11), kind=kOutput, calls=%fused_computation.1 | convolution fusion | flops 402751488 | bytes 1835012 | tf_op jit(solution)/shard_map/dot_general | solution.py:20
Async XLA Ops:
  6.5 28.9 %all-gather.2.cloned.1.call-start = ((), (), s32[]{:S(2)}) async-start(), calls=%async_computation | async-start | bytes 1179648 | tf_op jit(solution)/shard_map/all_gather | solution.py:36
  8.9 26.5 %copy-start.1 = (f32[128,256]{1,0:T(8,128)S(1)}, f32[128,256]{1,0:T(8,128)}, u32[]{:S(2)}) copy-start(f32[128,256]{1,0:T(8,128)} %broadcast_multiply_fusion) | copy-start | bytes 393220
  9.0 68.3 %all-reduce.2.cloned.1.call-start = ((), (), s32[]{:S(2)}) async-start(), calls=%async_computation.1 | async-start | bytes 1048576 | tf_op jit(solution)/shard_map/psum | solution.py:38
  35.5 41.8 %copy-start = (f32[1024,256]{1,0:T(8,128)S(1)}, f32[1024,256]{1,0:T(8,128)}, u32[]{:S(2)}) copy-start(f32[1024,256]{1,0:T(8,128)} %all-gather.2.cloned.1.call-done) | copy-start | bytes 3145732
Sparse Core Ops, SparseCore 0:
  9.2 26.1 all-gather.1
  38.9 38.2 all-reduce.1
where the time goes:
time: 86.6 us; the launch traced here: 86.4 us
  waiting for transfers between devices  64.9 us (75%)
  between operations  13.4 us (15%)
  matrix products  5.65 us (7%)
  other arithmetic  2.33 us (3%)
    psum x1, waiting for transfers between devices, on_device(): whole_rows = lax.psum(partial_value, 'layer')  38.4 us
    all_gather x1, waiting for transfers between devices, on_device(): gathered = lax.all_gather(masked, ('row', 'col'), axis=0, tiled=True)  26.5 us
    dot_general x1, matrix products, times_panel(): lax.dot_general(left, panel, (((1,), (1,)), ((), ())), precision=lax.Prec...  3.29 us
    dot_general x1, matrix products, times_rows(): jnp.dot(left, panel, precision=lax.Precision.HIGHEST, preferred_element_t...  2.36 us
  transfers between devices with their start and end apart: 2, of which 2 were waited for; matrix products, arithmetic and copies ran while one was open for 0% of the time, Pallas kernels for 0%

commit v1 on v0

v1 whole, which is shorter than its diff:
```python
import functools
import itertools

import jax
import jax.numpy as jnp
from jax import lax
from jax.experimental import pallas as pl
from jax.experimental.pallas import tpu as pltpu
from jax.sharding import PartitionSpec as P

TILE = 128
PAIR = 2


def split(value):
    high = value.astype(jnp.bfloat16)
    return high, (value - high.astype(jnp.float32)).astype(jnp.bfloat16)


def times(left, right):
    dot = functools.partial(jnp.dot, preferred_element_type=jnp.float32)
    return dot(left[0], right[0]) + (dot(left[0], right[1]) + dot(left[1], right[0]))


def kernel(
    layers, rows, cols, density_ref, pattern_ref, out_ref,
    panel, square, slabs, slab_sem, slab_send, panel_sem, panel_send,
):
    layer, row, col = (lax.axis_index(name) for name in ("layer", "row", "col"))
    height, width = density_ref.shape
    me = row * cols + col
    half = lax.rem(col, PAIR)
    mate_col = col + 1 - 2 * half
    mate = row * cols + mate_col
    groups = cols // PAIR
    offsets = sorted(itertools.product(range(rows), range(groups)), key=lambda at: -sum(map(bool, at)))
    offsets.remove((0, 0))

    def peer(dr, dc):
        return lax.rem(row + dr + rows, rows), lax.rem(col + PAIR * dc + cols, cols)

    barrier = pltpu.get_barrier_semaphore()

    def greet(**device):
        pl.semaphore_signal(barrier, inc=1, device_id=device, device_id_type=pl.DeviceIdType.MESH)

    greet(col=mate_col)
    for dr, dc in offsets:
        r, c = peer(dr, dc)
        greet(row=r, col=c)
    for step in range(1, layers):
        greet(layer=lax.rem(layer + step, layers))

    def block(buffer, index):
        return buffer.at[pl.ds(pl.multiple_of(index * height, height), height), :]

    own = block(panel, me)
    for i in range(height // TILE):
        for j in range(width // TILE):
            keep = pattern_ref[me * (height // TILE) + i, layer * (width // TILE) + j].astype(jnp.float32)
            part = (slice(i * TILE, (i + 1) * TILE), slice(j * TILE, (j + 1) * TILE))
            own[part] = density_ref[part] * keep

    pl.semaphore_wait(barrier, layers + len(offsets))

    def copy(source, target, send, recv, **device):
        return pltpu.make_async_remote_copy(
            src_ref=source, dst_ref=target, send_sem=send, recv_sem=recv,
            device_id=device, device_id_type=pl.DeviceIdType.MESH,
        )

    started = []

    def start(*args, **device):
        one = copy(*args, **device)
        one.start()
        started.append(one)

    def send_slabs():
        for step in range(1, layers):
            to = lax.rem(layer + step, layers)
            start(own, slabs.at[layer], slab_send.at[step - 1], slab_sem.at[layer], layer=to)

    def send_block(phase, buffer):
        mine = block(buffer, me)
        for k, (dr, dc) in enumerate(offsets):
            r, c = peer(dr, dc)
            start(mine, mine, panel_send.at[phase, k], panel_sem.at[phase, me], row=r, col=c)
        start(mine, mine, panel_send.at[phase, len(offsets)], panel_sem.at[phase, me], col=mate_col)

    def arrive(phase, buffer, index):
        there = block(buffer, index)
        copy(there, there, panel_send.at[phase, 0], panel_sem.at[phase, index], col=mate_col).wait_recv()

    def share(phase, buffer):
        for k, (dr, dc) in enumerate(reversed(offsets)):
            r, c = peer(-dr, -dc)
            source = r * cols + c
            arrive(phase, buffer, source)
            there = block(buffer, source)
            start(
                there, there, panel_send.at[phase, len(offsets) + 1 + k], panel_sem.at[phase, source],
                col=mate_col,
            )

    def collect(phase, buffer):
        arrive(phase, buffer, mate)
        for dr, dc in reversed(offsets):
            r, c = peer(-dr, -dc)
            arrive(phase, buffer, r * cols + c + 1 - 2 * half)

    def slab_of(buffer, index):
        return buffer[pl.ds(pl.multiple_of(index * width, width), width), :]

    send_block(0, panel)
    send_slabs()
    share(0, panel)
    slabs[layer] = own[...]
    collect(0, panel)
    total = times(split(own[...]), split(slab_of(panel, layer)))
    for step in range(1, layers):
        source = lax.rem(layer + layers - step, layers)
        here = slabs.at[source]
        copy(here, here, slab_send.at[0], slab_sem.at[source], layer=source).wait_recv()
        total += times(split(here[...]), split(slab_of(panel, source)))
    block(square, me)[...] = total
    send_block(1, square)
    share(1, square)
    collect(1, square)
    cube = times(split(slabs[0]), split(square[:width, :]))
    for index in range(1, layers):
        cube += times(split(slabs[index]), split(square[index * width : (index + 1) * width, :]))
    out_ref[...] = 3.0 * total - 2.0 * cube
    for one in started:
        one.wait_send()


def solution(mesh):
    layers, rows, cols = (mesh.shape[name] for name in ("layer", "row", "col"))

    def on_device(density, pattern):
        height, width = density.shape
        blocks = rows * cols
        sends = 2 * (blocks // PAIR)
        return pl.pallas_call(
            functools.partial(kernel, layers, rows, cols),
            out_shape=jax.ShapeDtypeStruct((height, width), jnp.float32),
            in_specs=[
                pl.BlockSpec(memory_space=pltpu.VMEM),
                pl.BlockSpec(memory_space=pltpu.SMEM),
            ],
            out_specs=pl.BlockSpec(memory_space=pltpu.VMEM),
            scratch_shapes=[
                pltpu.VMEM((blocks * height, width), jnp.float32),
                pltpu.VMEM((blocks * height, width), jnp.float32),
                pltpu.VMEM((layers, height, width), jnp.float32),
                pltpu.SemaphoreType.DMA((layers,)),
                pltpu.SemaphoreType.DMA((layers,)),
                pltpu.SemaphoreType.DMA((2, blocks)),
                pltpu.SemaphoreType.DMA((2, sends)),
            ],
            compiler_params=pltpu.CompilerParams(
                collective_id=0, has_side_effects=True, vmem_limit_bytes=40 * 2**20
            ),
        )(density, pattern)

    return jax.shard_map(
        on_device,
        mesh=mesh,
        in_specs=(P(("row", "col"), "layer"), P()),
        out_specs=P(("row", "col"), "layer"),
        check_vma=False,
    )
```

time: 86.6 us -> 28.7 us (0.33)
  the two profiles are of different devices: /device:TPU:0 before, /device:TPU:13 now
where the time goes in v1:
time: 28.7 us; the launch traced here: 28.5 us
  Pallas kernels  26.2 us (91%)
  local copies, waits for them, and re-layouts  2.25 us (8%)
    pallas_call x1, Pallas kernels, on_device(): pl.pallas_call(functools.partial(kernel, layers, rows, cols), out_shape=j...  26.2 us
    unnamed x5, local copies, waits for them, and re-layouts  2.25 us

profile of v1, /device:TPU:13, one launch (start us, length us, event | category | flops | bytes accessed | tf_op | source)
XLA Modules:
  0.0 28.5 jit_solution(18332660125449071157)
XLA Ops:
  0.0 0.0 copy-start
  0.0 0.9 %copy-done = f32[128,256]{1,0:T(8,128)S(1)} copy-done((f32[128,256]{1,0:T(8,128)S(1)}, f32[128,256]{1,0:T(8,128)}, u32[]{:S(2)}) %copy-start) | copy-done | bytes 131096
  0.9 0.0 copy-start.1
  0.9 0.7 %copy-done.1 = s32[8,8]{1,0:T(8,128)S(1)} copy-done((s32[8,8]{1,0:T(8,128)S(1)}, s32[8,8]{1,0:T(8,128)}, u32[]{:S(2)}) %copy-start.1) | copy-done | bytes 280
  1.6 26.2 %shard_map.28 = f32[128,256]{1,0:T(8,128)S(1)} custom-call(f32[128,256]{1,0:T(8,128)S(1)} %copy-done, s32[8,8]{1,0:T(8,128)S(1)} %copy-done.1), custom_call_target="tpu_custom_call" | custom-call | tf_op jit(solution)/shard_map/pallas_call | solution.py:145
  27.8 0.7 %copy.4 = f32[128,256]{1,0:T(8,128)} copy(f32[128,256]{1,0:T(8,128)S(1)} %shard_map.28) | data formatting | bytes 262144
Async XLA Ops:
  0.0 0.9 %copy-start = (f32[128,256]{1,0:T(8,128)S(1)}, f32[128,256]{1,0:T(8,128)}, u32[]{:S(2)}) copy-start(f32[128,256]{1,0:T(8,128)} %density_ref.1) | copy-start | bytes 393220
  0.9 0.7 %copy-start.1 = (s32[8,8]{1,0:T(8,128)S(1)}, s32[8,8]{1,0:T(8,128)}, u32[]{:S(2)}) copy-start(s32[8,8]{1,0:T(8,128)} %pattern_ref.1) | copy-start | bytes 772

commit v2 on v1

v2 whole, which is shorter than its diff:
```python
import functools
import itertools

import jax
import jax.numpy as jnp
from jax import lax
from jax.experimental import pallas as pl
from jax.experimental.pallas import tpu as pltpu
from jax.sharding import PartitionSpec as P

TILE = 128
CHUNKS = 1
REACH = 2
PAIR = 2


def split(value):
    high = value.astype(jnp.bfloat16)
    return high, (value - high.astype(jnp.float32)).astype(jnp.bfloat16)


def times(left, right):
    dot = functools.partial(jnp.dot, preferred_element_type=jnp.float32)
    return dot(left[0], right[0]) + (dot(left[0], right[1]) + dot(left[1], right[0]))


def kernel(
    layers, rows, cols, density_hbm, pattern_hbm, out_ref,
    density_ref, pattern_ref, panel, square, slabs,
    local_sem, slab_sem, slab_send, relay_send, panel_sem, panel_send,
):
    layer, row, col = (lax.axis_index(name) for name in ("layer", "row", "col"))
    height, width = density_ref.shape
    rise = height // CHUNKS
    me = row * cols + col
    half = lax.rem(col, PAIR)
    mate_col = col + 1 - 2 * half
    mate = row * cols + mate_col
    groups = cols // PAIR
    offsets = sorted(itertools.product(range(rows), range(groups)), key=lambda at: -sum(map(bool, at)))
    offsets.remove((0, 0))

    def peer(dr, dc):
        return lax.rem(row + dr + rows, rows), lax.rem(col + PAIR * dc + cols, cols)

    load = pltpu.make_async_copy(density_hbm, density_ref, local_sem.at[0])
    load.start()
    load_pattern = pltpu.make_async_copy(pattern_hbm, pattern_ref, local_sem.at[1])
    load_pattern.start()

    barrier = pltpu.get_barrier_semaphore()

    def greet(**device):
        pl.semaphore_signal(barrier, inc=1, device_id=device, device_id_type=pl.DeviceIdType.MESH)

    def inside(at):
        return (at >= 0) & (at < layers)

    reach = [sign * far for far in range(min(REACH, layers - 1), 0, -1) for sign in (1, -1)]
    known = jnp.int32(1 + len(offsets))
    greet(col=mate_col)
    for away in reach:
        pl.when(inside(layer + away))(functools.partial(greet, layer=layer + away))
        known += inside(layer + away).astype(jnp.int32)
    for dr, dc in offsets:
        r, c = peer(dr, dc)
        greet(row=r, col=c)

    def block(buffer, index):
        return buffer.at[pl.ds(pl.multiple_of(index * height, height), height), :]

    def piece(buffer, index, chunk):
        return buffer.at[pl.ds(pl.multiple_of(index * height + chunk * rise, rise), rise), :]

    own = block(panel, me)
    load_pattern.wait()
    load.wait()
    for i in range(height // TILE):
        for j in range(width // TILE):
            keep = pattern_ref[me * (height // TILE) + i, layer * (width // TILE) + j].astype(jnp.float32)
            part = (slice(i * TILE, (i + 1) * TILE), slice(j * TILE, (j + 1) * TILE))
            own[part] = density_ref[part] * keep

    pl.semaphore_wait(barrier, known)

    def copy(source, target, send, recv, **device):
        return pltpu.make_async_remote_copy(
            src_ref=source, dst_ref=target, send_sem=send, recv_sem=recv,
            device_id=device, device_id_type=pl.DeviceIdType.MESH,
        )

    started = []

    def start(when, *args, **device):
        one = copy(*args, **device)
        if when is None:
            one.start()
        else:
            pl.when(when)(one.start)
        started.append((when, one))

    def chunk_of(chunk):
        return pl.ds(chunk * rise, rise)

    def send_slab(chunk):
        for n, away in enumerate(reach):
            start(
                inside(layer + away),
                piece(panel, me, chunk), slabs.at[layer, chunk_of(chunk)],
                slab_send.at[chunk, n], slab_sem.at[chunk, layer], layer=layer + away,
            )

    def slab_arrives(chunk, source):
        there = slabs.at[source, chunk_of(chunk)]
        copy(there, there, slab_send.at[0, 0], slab_sem.at[chunk, source], layer=layer).wait_recv()

    relays = [(sign, hops) for hops in range(1, (layers - 2) // REACH + 1) for sign in (1, -1)]

    def relay_slab(chunk):
        for n, (sign, hops) in enumerate(relays):
            source = layer - sign * hops * REACH
            mine = inside(source) & inside(layer + sign)
            pl.when(mine)(functools.partial(slab_arrives, chunk, source))
            for far in range(REACH, 0, -1):
                there = slabs.at[source, chunk_of(chunk)]
                start(
                    inside(source) & inside(layer + sign * far),
                    there, there, relay_send.at[chunk, n, far - 1], slab_sem.at[chunk, source],
                    layer=layer + sign * far,
                )

    def relayed(source):
        below = (source < layer) & (layer + 1 < layers)
        above = (source > layer) & (layer > 0)
        return (lax.rem(lax.abs(source - layer), REACH) == 0) & (below | above)

    def send_piece(phase, mine):
        for k, (dr, dc) in enumerate(offsets):
            r, c = peer(dr, dc)
            start(None, mine, mine, panel_send.at[phase, k], panel_sem.at[phase, me], row=r, col=c)
        start(None, mine, mine, panel_send.at[phase, len(offsets)], panel_sem.at[phase, me], col=mate_col)

    def arrive(phase, there, index):
        copy(there, there, panel_send.at[phase, 0], panel_sem.at[phase, index], col=mate_col).wait_recv()

    def share(phase, at):
        for k, (dr, dc) in enumerate(reversed(offsets)):
            r, c = peer(-dr, -dc)
            source = r * cols + c
            there = at(source)
            arrive(phase, there, source)
            start(
                None, there, there, panel_send.at[phase, len(offsets) + 1 + k],
                panel_sem.at[phase, source], col=mate_col,
            )

    def collect(phase, at):
        arrive(phase, at(mate), mate)
        for dr, dc in reversed(offsets):
            r, c = peer(-dr, -dc)
            source = r * cols + c + 1 - 2 * half
            arrive(phase, at(source), source)

    def slab_of(buffer, index):
        return buffer[pl.ds(pl.multiple_of(index * width, width), width), :]

    whole = functools.partial(block, panel)
    parts = [functools.partial(piece, square, chunk=chunk) for chunk in range(CHUNKS)]

    send_slab(0)
    send_piece(0, own)
    for chunk in range(1, CHUNKS):
        send_slab(chunk)
    slabs[layer] = own[...]
    relay_slab(0)
    share(0, whole)
    for chunk in range(1, CHUNKS - 1):
        relay_slab(chunk)
    collect(0, whole)
    for chunk in range(CHUNKS):
        if 0 < chunk == CHUNKS - 1:
            relay_slab(chunk)
        total = times(split(slabs[layer, chunk_of(chunk)]), split(slab_of(panel, layer)))
        for step in range(1, layers):
            source = lax.rem(layer + layers - step, layers)
            pl.when(jnp.logical_not(relayed(source)))(functools.partial(slab_arrives, chunk, source))
            total += times(split(slabs[source, chunk_of(chunk)]), split(slab_of(panel, source)))
        piece(square, me, chunk)[...] = total
        send_piece(1 + chunk, piece(square, me, chunk))
        if chunk:
            share(chunk, parts[chunk - 1])
    share(CHUNKS, parts[-1])
    for chunk in range(CHUNKS):
        collect(1 + chunk, parts[chunk])
    cube = times(split(slabs[0]), split(square[:width, :]))
    for index in range(1, layers):
        cube += times(split(slabs[index]), split(square[index * width : (index + 1) * width, :]))
    out_ref[...] = 3.0 * block(square, me)[...] - 2.0 * cube
    for when, one in started:
        if when is None:
            one.wait_send()
        else:
            pl.when(when)(one.wait_send)


def solution(mesh):
    layers, rows, cols = (mesh.shape[name] for name in ("layer", "row", "col"))

    def on_device(density, pattern):
        height, width = density.shape
        blocks = rows * cols
        sends = 2 * (blocks // PAIR)
        return pl.pallas_call(
            functools.partial(kernel, layers, rows, cols),
            out_shape=jax.ShapeDtypeStruct((height, width), jnp.float32),
            in_specs=[
                pl.BlockSpec(memory_space=pltpu.HBM),
                pl.BlockSpec(memory_space=pltpu.HBM),
            ],
            out_specs=pl.BlockSpec(memory_space=pltpu.VMEM),
            scratch_shapes=[
                pltpu.VMEM((height, width), jnp.float32),
                pltpu.SMEM(pattern.shape, jnp.int32),
                pltpu.VMEM((blocks * height, width), jnp.float32),
                pltpu.VMEM((blocks * height, width), jnp.float32),
                pltpu.VMEM((layers, height, width), jnp.float32),
                pltpu.SemaphoreType.DMA((2,)),
                pltpu.SemaphoreType.DMA((CHUNKS, layers)),
                pltpu.SemaphoreType.DMA((CHUNKS, 2 * REACH)),
                pltpu.SemaphoreType.DMA((CHUNKS, layers, REACH)),
                pltpu.SemaphoreType.DMA((1 + CHUNKS, blocks)),
                pltpu.SemaphoreType.DMA((1 + CHUNKS, sends)),
            ],
            compiler_params=pltpu.CompilerParams(
                collective_id=0, has_side_effects=True, vmem_limit_bytes=40 * 2**20
            ),
        )(density, pattern)

    return jax.shard_map(
        on_device,
        mesh=mesh,
        in_specs=(P(("row", "col"), "layer"), P()),
        out_specs=P(("row", "col"), "layer"),
        check_vma=False,
    )
```

time: 28.7 us -> 26.7 us (0.930)
  the two profiles are of different devices: /device:TPU:13 before, /device:TPU:1 now
where the time goes in v2:
time: 26.7 us; the launch traced here: 26.5 us
  Pallas kernels  24.3 us (91%)
  local copies, waits for them, and re-layouts  2.25 us (8%)
    pallas_call x1, Pallas kernels, on_device(): pl.pallas_call(functools.partial(kernel, layers, rows, cols), out_shape=j...  24.3 us
    unnamed x5, local copies, waits for them, and re-layouts  2.25 us

profile of v2, /device:TPU:1, one launch (start us, length us, event | category | flops | bytes accessed | tf_op | source)
XLA Modules:
  0.0 26.5 jit_solution(2933341704518885096)
XLA Ops:
  0.0 0.0 copy-start
  0.0 0.9 %copy-done = f32[128,256]{1,0:T(8,128)S(1)} copy-done((f32[128,256]{1,0:T(8,128)S(1)}, f32[128,256]{1,0:T(8,128)}, u32[]{:S(2)}) %copy-start) | copy-done | bytes 131096
  0.9 0.0 copy-start.1
  0.9 0.7 %copy-done.1 = s32[8,8]{1,0:T(8,128)S(1)} copy-done((s32[8,8]{1,0:T(8,128)S(1)}, s32[8,8]{1,0:T(8,128)}, u32[]{:S(2)}) %copy-start.1) | copy-done | bytes 280
  1.6 24.3 %shard_map.28 = f32[128,256]{1,0:T(8,128)S(1)} custom-call(f32[128,256]{1,0:T(8,128)S(1)} %copy-done, s32[8,8]{1,0:T(8,128)S(1)} %copy-done.1), custom_call_target="tpu_custom_call" | custom-call | tf_op jit(solution)/shard_map/pallas_call | solution.py:213
  25.9 0.7 %copy.4 = f32[128,256]{1,0:T(8,128)} copy(f32[128,256]{1,0:T(8,128)S(1)} %shard_map.28) | data formatting | bytes 262144
Async XLA Ops:
  0.0 0.9 %copy-start = (f32[128,256]{1,0:T(8,128)S(1)}, f32[128,256]{1,0:T(8,128)}, u32[]{:S(2)}) copy-start(f32[128,256]{1,0:T(8,128)} %density_hbm.1) | copy-start | bytes 393220
  0.9 0.7 %copy-start.1 = (s32[8,8]{1,0:T(8,128)S(1)}, s32[8,8]{1,0:T(8,128)}, u32[]{:S(2)}) copy-start(s32[8,8]{1,0:T(8,128)} %pattern_hbm.1) | copy-start | bytes 772

commit v3 on v2

--- a/solution.py
+++ b/solution.py
@@ -189,12 +189,26 @@
         send_piece(1 + chunk, piece(square, me, chunk))
         if chunk:
             share(chunk, parts[chunk - 1])
+    def term(first):
+        left = jnp.concatenate(
+            [
+                slabs[lax.div(first + n, width // height), :, pl.ds(pl.multiple_of(lax.rem(first + n, width // height) * height, TILE), height)]
+                for n in range(PAIR)
+            ],
+            axis=1,
+        )
+        return times(split(left), split(square[pl.ds(pl.multiple_of(first * height, height), PAIR * height), :]))
+
+    for chunk in range(CHUNKS):
+        arrive(1 + chunk, parts[chunk](mate), mate)
+    cube = term(me - half)
     share(CHUNKS, parts[-1])
-    for chunk in range(CHUNKS):
-        collect(1 + chunk, parts[chunk])
-    cube = times(split(slabs[0]), split(square[:width, :]))
-    for index in range(1, layers):
-        cube += times(split(slabs[index]), split(square[index * width : (index + 1) * width, :]))
+    for dr, dc in reversed(offsets):
+        r, c = peer(-dr, -dc)
+        source = r * cols + c + 1 - 2 * half
+        for chunk in range(CHUNKS):
+            arrive(1 + chunk, parts[chunk](source), source)
+        cube += term(r * cols + c - half)
     out_ref[...] = 3.0 * block(square, me)[...] - 2.0 * cube
     for when, one in started:
         if when is None:

time: 26.7 us -> 26.4 us (0.989)
  Pallas kernels: 24.3 us -> 24 us
    pallas_call x1, Pallas kernels: 24.3 us -> 24 us  [on_device(): pl.pallas_call(functools.partial(kernel, layers, rows, cols), out_shape=j...]
where the time goes in v3:
time: 26.4 us; the launch traced here: 26.2 us
  Pallas kernels  24 us (91%)
  local copies, waits for them, and re-layouts  2.25 us (9%)
    pallas_call x1, Pallas kernels, on_device(): pl.pallas_call(functools.partial(kernel, layers, rows, cols), out_shape=j...  24 us
    unnamed x5, local copies, waits for them, and re-layouts  2.25 us

profile of v3, /device:TPU:1, one launch (start us, length us, event | category | flops | bytes accessed | tf_op | source)
XLA Modules:
  0.0 26.2 jit_solution(17160753099159488769)
XLA Ops:
  0.0 0.0 copy-start
  0.0 0.9 %copy-done = f32[128,256]{1,0:T(8,128)S(1)} copy-done((f32[128,256]{1,0:T(8,128)S(1)}, f32[128,256]{1,0:T(8,128)}, u32[]{:S(2)}) %copy-start) | copy-done | bytes 131096
  0.9 0.0 copy-start.1
  0.9 0.7 %copy-done.1 = s32[8,8]{1,0:T(8,128)S(1)} copy-done((s32[8,8]{1,0:T(8,128)S(1)}, s32[8,8]{1,0:T(8,128)}, u32[]{:S(2)}) %copy-start.1) | copy-done | bytes 280
  1.6 24.0 %shard_map.28 = f32[128,256]{1,0:T(8,128)S(1)} custom-call(f32[128,256]{1,0:T(8,128)S(1)} %copy-done, s32[8,8]{1,0:T(8,128)S(1)} %copy-done.1), custom_call_target="tpu_custom_call" | custom-call | tf_op jit(solution)/shard_map/pallas_call | solution.py:227
  25.6 0.7 %copy.4 = f32[128,256]{1,0:T(8,128)} copy(f32[128,256]{1,0:T(8,128)S(1)} %shard_map.28) | data formatting | bytes 262144
Async XLA Ops:
  0.0 0.9 %copy-start = (f32[128,256]{1,0:T(8,128)S(1)}, f32[128,256]{1,0:T(8,128)}, u32[]{:S(2)}) copy-start(f32[128,256]{1,0:T(8,128)} %density_hbm.1) | copy-start | bytes 393220
  0.9 0.7 %copy-start.1 = (s32[8,8]{1,0:T(8,128)S(1)}, s32[8,8]{1,0:T(8,128)}, u32[]{:S(2)}) copy-start(s32[8,8]{1,0:T(8,128)} %pattern_hbm.1) | copy-start | bytes 772
